TPU v7x, 256 devices: a whole 4x4x8 slice. The times are simulated.
256 devices in a mesh: blk: 16 (over y, z_lo), grp: 16 (over z_hi, x, core).
Axes of the slice: x: 4, y: 4, z: 8 (z_hi: 2, z_lo: 4; z = z_hi * 4 + z_lo), core: 2. Of those that a mesh axis runs over, the one named last changes fastest.
Arguments:
- images: bfloat16 [32768, 1152], P(('blk', 'grp')), may hold values from -0.1875 to 0.1875
- text_embed: bfloat16 [32768, 1152], P(('blk', 'grp')), may hold values from -0.1875 to 0.1875
- log_scale: float32 [1], replicated, may hold values from 3 to 4
- logit_bias: float32 [1], replicated, may hold values from -6 to -3
Outputs:
- image_grad: float32 [32768, 1152], P(('blk', 'grp'))
- text_grad: float32 [32768, 1152], P(('blk', 'grp'))
All inputs are finite; a program needn't handle non-finite values.
Results may differ from a plain program's by a relative error of at most 0.0063.
Values may be sent and summed in bfloat16 or wider, within the bound.
A program may use at most 128 MiB of HBM per device.

v0:
```python
import jax
import jax.numpy as jnp
from jax import lax
from jax.sharding import PartitionSpec as P

EPS = 1e-06


def from_behind(x, axis, by):
    count = lax.axis_size(axis)
    return lax.ppermute(x, axis, [(i, (i + by) % count) for i in range(count)])


def unitize(embed):
    values = embed.astype(jnp.float32)
    inverse = lax.rsqrt(jnp.sum(values * values, axis=-1, keepdims=True) + EPS)
    return (values * inverse, inverse)


def project_back(grad_hat, unit_rows, inverse):
    inner = jnp.sum(grad_hat * unit_rows, axis=-1, keepdims=True)
    return inverse * (grad_hat - inner * unit_rows)


def per_device(images, text_embed, log_scale, logit_bias):
    temper = jnp.exp(log_scale[0])
    offset = logit_bias[0]
    row_count = images.shape[0]
    img_unit, img_inverse = unitize(images)
    txt_unit, txt_inverse = unitize(text_embed)
    img_hat = img_unit.astype(jnp.bfloat16)
    txt_hat = txt_unit.astype(jnp.bfloat16)
    own_block = lax.all_gather(txt_hat, "grp", axis=0, tiled=True)
    next_block = from_behind(own_block, "blk", 1)
    member = lax.axis_index("grp")
    local_rows = lax.broadcasted_iota(jnp.int32, (row_count, own_block.shape[0]), 0)
    block_cols = lax.broadcasted_iota(jnp.int32, (row_count, own_block.shape[0]), 1)
    positive = (block_cols == member * row_count + local_rows).astype(jnp.float32)

    def pair_weights(rows_here, block, target):
        logits = (
            temper
            * lax.dot_general(
                rows_here, block, (((1,), (1,)), ((), ())), preferred_element_type=jnp.float32
            )
            + offset
        )
        return (temper * (jax.nn.sigmoid(logits) - target)).astype(jnp.bfloat16)

    own_weights = pair_weights(img_hat, own_block, positive)
    next_weights = pair_weights(img_hat, next_block, 0.0)
    img_grad_hat = jnp.dot(own_weights, own_block, preferred_element_type=jnp.float32) + jnp.dot(
        next_weights, next_block, preferred_element_type=jnp.float32
    )
    own_partial = lax.dot_general(
        own_weights, img_hat, (((0,), (0,)), ((), ())), preferred_element_type=jnp.float32
    )
    next_partial = lax.dot_general(
        next_weights, img_hat, (((0,), (0,)), ((), ())), preferred_element_type=jnp.float32
    )
    own_total = lax.psum_scatter(own_partial, "grp", scatter_dimension=0, tiled=True)
    next_total = lax.psum_scatter(next_partial, "grp", scatter_dimension=0, tiled=True)
    txt_grad_hat = own_total + from_behind(next_total, "blk", -1)
    image_grad = project_back(img_grad_hat, img_unit, img_inverse)
    text_grad = project_back(txt_grad_hat, txt_unit, txt_inverse)
    return (image_grad, text_grad)


def solution(mesh):
    in_specs = (P(("blk", "grp"), None), P(("blk", "grp"), None), P(), P())
    out_specs = (P(("blk", "grp"), None), P(("blk", "grp"), None))
    return jax.shard_map(
        per_device, mesh=mesh, in_specs=in_specs, out_specs=out_specs, check_vma=False
    )
```

profile of v0, /device:TPU:1, one launch (start us, length us, event | category | flops | bytes accessed | tf_op | source)
XLA Modules:
  0.0 518.2 jit_solution(15246078626406128725)
XLA Ops:
  7.2 0.0 all-gather.2.cloned.1.call-start
  7.2 1.1 fusion.28
  8.3 1.8 fusion.17
  10.1 0.0 all-gather.2.cloned.1.call-update
  10.1 0.0 reduce-scatter.5.cloned.1.call-start
  10.2 86.4 %all-gather.2.cloned.1.call-done = bf16[2048,1152]{1,0:T(8,128)(2,1)} async-done(((bf16[128,1152]{1,0:T(8,128)(2,1)}), bf16[2048,1152]{1,0:T(8,128)(2,1)}) %all-gather.2.cloned.1.call-update) | async-done | bytes 4718608 | tf_op jit(solution)/shard_map/all_gather | solution.py:33
  96.6 0.2 collective-permute-start
  98.2 1.1 fusion.24
  99.3 104.6 %collective-permute-done = bf16[2048,1152]{1,0:T(8,128)(2,1)S(1)} collective-permute-done((bf16[2048,1152]{1,0:T(8,128)(2,1)}, bf16[2048,1152]{1,0:T(8,128)(2,1)S(1)}, u32[]{:S(2)}, u32[]{:S(2)}) %collective-permute-start) | collective-permute-done | bytes 4718624 | tf_op jit(solution)/shard_map/ppermute | solution.py:11
  203.8 0.0 copy-start.2
  203.8 0.0 copy-start
  203.8 2.9 fusion.14
  206.8 0.0 copy-done.2
  206.8 0.0 copy-done
  206.8 5.1 fusion.29
  211.9 0.0 reduce-scatter.5.cloned.1.call-update
  212.0 0.0 reduce-scatter.3.cloned.1.call-start
  212.0 4.1 fusion.13
  216.1 5.3 %fusion.31 = f32[2048,1152]{1,0:T(8,128)} fusion(bf16[128,2048]{1,0:T(8,128)(2,1)S(1)} %fusion.13, bf16[128,1152]{1,0:T(8,128)(2,1)S(1)} %copy-done, f32[128]{0:T(128)S(1)} %add_rsqrt_fusion.1), kind=kOutput, calls=%fused_computation.41 | convolution fusion | flops 604422144 | bytes 10256896 | tf_op jit(solution)/shard_map/dot_general | solution.py:55
  221.4 0.0 reduce-scatter.3.cloned.1.call-update
  221.4 3.8 fusion.35
  225.2 0.0 copy-start.1
  225.2 132.1 %reduce-scatter.5.cloned.1.call-done = f32[128,1152]{1,0:T(8,128)} async-done(((f32[2048,1152]{1,0:T(8,128)}), f32[128,1152]{1,0:T(8,128)}) %reduce-scatter.5.cloned.1.call-update) | async-done | bytes 589840 | tf_op jit(solution)/shard_map/reduce_scatter | solution.py:62
  357.3 2.6 collective-permute-start.1
  359.8 3.3 fusion.21
  363.2 1.0 fusion.23
  364.2 145.1 %reduce-scatter.3.cloned.1.call-done = f32[128,1152]{1,0:T(8,128)} async-done(((f32[2048,1152]{1,0:T(8,128)}), f32[128,1152]{1,0:T(8,128)}) %reduce-scatter.3.cloned.1.call-update) | async-done | bytes 589840 | tf_op jit(solution)/shard_map/reduce_scatter | solution.py:61
  509.3 0.0 collective-permute-done.1
  509.3 0.0 copy-done.1
  509.3 1.3 fusion.25
  510.6 1.0 fusion.27
  (3 shorter events, 0.0 us)
Async XLA Ops:
  7.2 89.4 %all-gather.2.cloned.1.call-start = ((), (), s32[]{:S(2)}) async-start(), calls=%async_computation.2 | async-start | bytes 5013504 | tf_op jit(solution)/shard_map/all_gather | solution.py:33
  10.1 347.1 %reduce-scatter.5.cloned.1.call-start = ((), (), s32[]{:S(2)}) async-start(), calls=%async_computation.4 | async-start | bytes 10027008 | tf_op jit(solution)/shard_map/reduce_scatter | solution.py:62
  96.6 107.3 %collective-permute-start = (bf16[2048,1152]{1,0:T(8,128)(2,1)}, bf16[2048,1152]{1,0:T(8,128)(2,1)S(1)}, u32[]{:S(2)}, u32[]{:S(2)}) collective-permute-start(bf16[2048,1152]{1,0:T(8,128)(2,1)} %all-gather.2.cloned.1.call-done), channel_id=1, source_target_pairs={{0,16},{16,32},{32,48},{48,64},{64,80},{80,96},{96,112},{112,128},... | collective-permute-start | bytes 14155784 | tf_op jit(solution)/shard_map/ppermute | solution.py:11
  203.8 3.0 copy-start.2
  203.8 3.0 copy-start
  212.0 297.3 %reduce-scatter.3.cloned.1.call-start = ((), (), s32[]{:S(2)}) async-start(), calls=%async_computation.3 | async-start | bytes 10027008 | tf_op jit(solution)/shard_map/reduce_scatter | solution.py:61
  225.2 284.1 %copy-start.1 = (bf16[128,1152]{1,0:T(8,128)(2,1)S(1)}, bf16[128,1152]{1,0:T(8,128)(2,1)}, u32[]{:S(2)}) copy-start(bf16[128,1152]{1,0:T(8,128)(2,1)} %param.5) | copy-start | bytes 884740
  357.3 152.1 %collective-permute-start.1 = (f32[128,1152]{1,0:T(8,128)}, f32[128,1152]{1,0:T(8,128)S(1)}, u32[]{:S(2)}, u32[]{:S(2)}) collective-permute-start(f32[128,1152]{1,0:T(8,128)} %reduce-scatter.5.cloned.1.call-done), channel_id=1, source_target_pairs={{0,240},{16,0},{32,16},{48,32},{64,48},{80,64},{96,80},{112,96},{1... | collective-permute-start | bytes 1769480 | tf_op jit(solution)/shard_map/ppermute | solution.py:11
Sparse Core Ops, SparseCore 0:
  11.3 85.2 all-gather.1
  212.1 145.1 reduce-scatter.4
  362.0 147.2 reduce-scatter.2
where the time goes:
time: 519 us; the launch traced here: 518 us
  waiting for transfers between devices  468 us (90%)
  matrix products  24.5 us (5%)
  between operations  15.1 us (3%)
  other arithmetic  7.42 us (1%)
    reduce_scatter x1, waiting for transfers between devices, per_device(): lax.psum_scatter(own_partial, 'grp', scatter_dimension=0, tiled=True)  145 us
    reduce_scatter x1, waiting for transfers between devices, per_device(): lax.psum_scatter(next_partial, 'grp', scatter_dimension=0, tiled=True)  132 us
    ppermute x2, waiting for transfers between devices, from_behind(): return lax.ppermute(x, axis, [(i, (i + by) % count) for i in range(count)])  105 us
    all_gather x1, waiting for transfers between devices, per_device(): own_block = lax.all_gather(txt_hat, 'grp', axis=0, tiled=True)  86.4 us
  transfers between devices with their start and end apart: 5, of which 4 were waited for; matrix products, arithmetic and copies ran while one was open for 4% of the time, Pallas kernels for 0%

commit v1 on v0

v1 whole, which is shorter than its diff:
```python
import functools

import jax
import jax.numpy as jnp
from jax import lax
from jax.experimental import pallas as pl
from jax.experimental.pallas import tpu as pltpu
from jax.sharding import PartitionSpec as P

EPS = 1e-06
R = 128
NX, NY, NZ = 4, 4, 8

SLOT = {2: 0, 1: 1, 3: 2, 0: 3}
FB = 80
RA = 48
FA = R - FB
OWN, P1 = 0, R
P2B, QA = 2 * R, 2 * R + FB
P2A, QB = 3 * R, 3 * R + FA


def kernel(
    img_hbm, txt_hbm, ls_ref, lb_ref, oimg_ref, otxt_ref,
    raw_img, raw_txt, imgs, txts, w_ref, wt_ref, dt_f, dt_b, back_in, own_in, far_in,
    di_f, di_out, di_in, xs, xh_in, xf_in, in_sem, send_sem, recv_sem,
):
    blk = lax.axis_index("blk")
    grp = lax.axis_index("grp")
    core = lax.rem(grp, 2)
    x = lax.rem(grp // 2, NX)
    z = lax.rem(blk, 4) + 4 * (grp // 8)

    def at(dblk, dz, dx=0, dcore=0):
        new_z = lax.rem(z + dz, NZ)
        new_x = lax.rem(x + dx, NX)
        new_core = lax.rem(core + dcore, 2)
        return (lax.rem(blk + dblk, 16), (new_z // 4 * NX + new_x) * 2 + new_core)

    near, near_back = at(1, 1), at(15, 7)
    far, far_back = at(1, 5), at(15, 3)
    right, left, twin = at(0, 0, 1), at(0, 0, 3), at(0, 0, 0, 1)

    load_txt = pltpu.make_async_copy(txt_hbm, raw_txt, in_sem.at[0])
    load_img = pltpu.make_async_copy(img_hbm, raw_img, in_sem.at[1])
    load_txt.start()
    load_img.start()
    barrier = pltpu.get_barrier_semaphore()
    peers = (near, near_back, far, far_back, right, left, twin)
    for peer in peers:
        pl.semaphore_signal(barrier, inc=1, device_id=peer, device_id_type=pl.DeviceIdType.MESH)

    copies = {}

    def send(name, src, dst, to):
        k = len(copies)
        copies[name] = pltpu.make_async_remote_copy(
            src_ref=src, dst_ref=dst, send_sem=send_sem.at[k], recv_sem=recv_sem.at[k],
            device_id=to, device_id_type=pl.DeviceIdType.MESH,
        )
        copies[name].start()

    def arrived(*names):
        for name in names:
            copies[name].wait_recv()

    def rows(ref, start, count):
        return ref.at[pl.ds(start, count)]

    def inverse_norm(raw):
        values = raw[...].astype(jnp.float32)
        return values, lax.rsqrt(jnp.sum(values * values, axis=-1, keepdims=True) + EPS)

    load_txt.wait()
    values, inverse = inverse_norm(raw_txt)
    txts[OWN:R, :] = (values * inverse).astype(jnp.bfloat16)
    pl.semaphore_wait(barrier, len(peers))

    send("n_a", rows(txts, FB, FA), rows(txts, P1 + FB, FA), near)
    send("f_b", rows(txts, 0, FB), rows(txts, P2B, FB), far)
    send("n_b", rows(txts, 0, FB), rows(txts, P1, FB), near)

    load_img.wait()
    values, inverse = inverse_norm(raw_img)
    imgs[7 * R : 8 * R, :] = (values * inverse).astype(jnp.bfloat16)

    def mine(dx):
        return (4 + SLOT[dx]) * R

    def other(dx):
        return SLOT[dx] * R

    half = R // 2
    send("r_lo", rows(imgs, mine(0), half), rows(imgs, mine(3), half), right)
    send("l_hi", rows(imgs, mine(0) + half, half), rows(imgs, mine(1) + half, half), left)
    send("r_hi", rows(imgs, mine(0) + half, half), rows(imgs, mine(3) + half, half), right)
    send("l_lo", rows(imgs, mine(0), half), rows(imgs, mine(1), half), left)
    send("t_0", rows(imgs, mine(0), R), rows(imgs, other(0), R), twin)

    arrived("n_a")
    send("o_a", rows(txts, P1 + FB, FA), rows(txts, QA, FA), far_back)
    arrived("r_lo")
    send("r2", rows(imgs, mine(3), half), rows(imgs, mine(2), half), right)
    arrived("l_hi")
    send("l2", rows(imgs, mine(1) + half, half), rows(imgs, mine(2) + half, half), left)
    arrived("r_hi")
    send("t_3", rows(imgs, mine(3), R), rows(imgs, other(3), R), twin)
    arrived("l_lo")
    send("t_1", rows(imgs, mine(1), R), rows(imgs, other(1), R), twin)
    arrived("f_b")
    send("o_b", rows(txts, P2B, FB), rows(txts, QB, FB), near_back)
    arrived("r2", "l2")
    send("t_2", rows(imgs, mine(2), R), rows(imgs, other(2), R), twin)
    arrived("o_a")
    send("f_a", rows(txts, QA, FA), rows(txts, P2A, FA), near)

    temper = jnp.exp(jnp.full((1, 256), ls_ref[0], jnp.float32))
    offset = jnp.full((1, 256), lb_ref[0], jnp.float32)

    def score(start, count, with_label):
        def tile(j, carry):
            cols = pl.ds(pl.multiple_of(j * 256, 256), 256)
            logits = lax.dot_general(
                txts[start : start + count, :], imgs[cols, :], (((1,), (1,)), ((), ())),
                preferred_element_type=jnp.float32,
            )
            weight = jax.nn.sigmoid(temper * logits + offset)
            if with_label:
                row = lax.broadcasted_iota(jnp.int32, (count, 256), 0) + (start + 7 * R)
                col = lax.broadcasted_iota(jnp.int32, (count, 256), 1) + j * 256
                weight = weight - (row == col).astype(jnp.float32)
            weight = (temper * weight).astype(jnp.bfloat16)
            w_ref[start : start + count, cols] = weight
            wt_ref[cols, start : start + count] = weight.T
            return carry

        lax.fori_loop(0, 4, tile, 0)

        def columns(cols):
            grad = jnp.dot(
                w_ref[start : start + count, :], imgs[:, cols], preferred_element_type=jnp.float32
            )
            dt_f[start : start + count, cols] = grad
            dt_b[start : start + count, cols] = grad.astype(jnp.bfloat16)

        def column_tile(j, carry):
            columns(pl.ds(pl.multiple_of(j * 256, 256), 256))
            return carry

        lax.fori_loop(0, 4, column_tile, 0)
        columns(pl.ds(1024, 128))

    def image_grads(pair, store):
        def columns(cols):
            store(cols, jnp.dot(
                wt_ref[pair * 256 : pair * 256 + 256, :], txts[:, cols],
                preferred_element_type=jnp.float32,
            ))

        def column_tile(j, carry):
            columns(pl.ds(pl.multiple_of(j * 256, 256), 256))
            return carry

        lax.fori_loop(0, 4, column_tile, 0)
        columns(pl.ds(1024, 128))

    def join(start, count, received):
        dt_b[start : start + count, :] = (
            dt_f[start : start + count, :] + received.astype(jnp.float32)
        ).astype(jnp.bfloat16)

    arrived("t_0", "t_3", "t_1", "t_2", "n_b")
    score(OWN, 2 * R, True)
    send("b_n", rows(dt_b, P1 + RA, R - RA), rows(own_in, RA, R - RA), near_back)

    score(P2B, R, False)
    send("b_fo", rows(dt_b, P2B, RA), rows(back_in, 0, RA), near_back)
    send("b_of_a", rows(dt_b, QA, FA), rows(back_in, 2 * RA + FB - RA, FA), near)

    arrived("o_b", "f_a")
    score(P2A, R, False)
    send("b_of_c", rows(dt_b, QB + RA, FB - RA), rows(back_in, 2 * RA, FB - RA), near)
    arrived("b_fo")
    join(QB, RA, back_in[0:RA, :])
    send("b_on", rows(dt_b, QB, RA), rows(back_in, RA, RA), far)
    arrived("b_of_a")
    join(P2A, FA, back_in[2 * RA + FB - RA : 2 * RA + R - RA, :])
    send("b_f_a", rows(dt_b, P2A, FA), rows(far_in, FB - RA, FA), far_back)

    def store_out(base):
        def store(cols, grad):
            di_out[base : base + 256, cols] = grad.astype(jnp.bfloat16)
        return store

    def store_keep(base):
        def store(cols, grad):
            di_f[base : base + 256, cols] = grad
        return store

    image_grads(0, store_out(0))
    send("c_2", rows(di_out, 0, R), rows(di_in, 0, R), twin)
    send("c_1", rows(di_out, R, R), rows(di_in, R, R), twin)
    arrived("b_of_c")
    join(P2B + RA, FB - RA, back_in[2 * RA : 2 * RA + FB - RA, :])
    send("b_f_c", rows(dt_b, P2B + RA, FB - RA), rows(far_in, 0, FB - RA), far_back)
    image_grads(1, store_out(2 * R))
    send("c_3", rows(di_out, 2 * R, R), rows(di_in, 2 * R, R), twin)
    send("c_0", rows(di_out, 3 * R, R), rows(di_in, 3 * R, R), twin)
    image_grads(2, store_keep(0))

    def both(start, count):
        return di_f[start : start + count, :] + di_in[start : start + count, :].astype(jnp.float32)

    arrived("c_2")
    xs[0:R, :] = both(0, R).astype(jnp.bfloat16)
    send("x2_r", rows(xs, 0, half), rows(xh_in, 0, half), right)
    send("x2_l", rows(xs, half, half), rows(xh_in, half, half), left)
    arrived("c_1")
    xs[R + half : 2 * R, :] = both(R + half, half).astype(jnp.bfloat16)
    send("x1_hi", rows(xs, R + half, half), rows(xf_in, half, half), right)
    image_grads(3, store_keep(2 * R))
    arrived("c_3")
    xs[2 * R : 2 * R + half, :] = both(2 * R, half).astype(jnp.bfloat16)
    send("x3_lo", rows(xs, 2 * R, half), rows(xf_in, R, half), left)
    arrived("x2_r")
    xs[R : R + half, :] = (both(R, half) + xh_in[0:half, :].astype(jnp.float32)).astype(jnp.bfloat16)
    send("x1_lo", rows(xs, R, half), rows(xf_in, 0, half), right)
    arrived("x2_l")
    xs[2 * R + half : 3 * R, :] = (
        both(2 * R + half, half) + xh_in[half:R, :].astype(jnp.float32)
    ).astype(jnp.bfloat16)
    send("x3_hi", rows(xs, 2 * R + half, half), rows(xf_in, R + half, half), left)

    arrived("b_on")
    join(P1, RA, back_in[RA : 2 * RA, :])
    send("b_n_a", rows(dt_b, P1, RA), rows(own_in, 0, RA), near_back)

    def project(raw, grad_hat):
        values, inverse = inverse_norm(raw)
        unit = values * inverse
        inner = jnp.sum(grad_hat * unit, axis=-1, keepdims=True)
        return inverse * (grad_hat - inner * unit)

    arrived("c_0", "x1_hi", "x3_lo", "x1_lo", "x3_hi")
    grad = both(3 * R, R) + xf_in[0:R, :].astype(jnp.float32) + xf_in[R : 2 * R, :].astype(jnp.float32)
    oimg_ref[...] = project(raw_img, grad)

    arrived("b_n", "b_f_a", "b_f_c", "b_n_a")
    dt_f[RA:R, :] = dt_f[RA:R, :] + far_in[...].astype(jnp.float32)
    otxt_ref[...] = project(raw_txt, dt_f[0:R, :] + own_in[...].astype(jnp.float32))
    for copy in copies.values():
        copy.wait_send()


def per_device(images, text_embed, log_scale, logit_bias):
    d = images.shape[1]
    bf, f32 = jnp.bfloat16, jnp.float32
    vmem, smem, hbm = (pl.BlockSpec(memory_space=m) for m in (pltpu.VMEM, pltpu.SMEM, pl.ANY))
    n_copies = 40
    return pl.pallas_call(
        kernel,
        out_shape=(jax.ShapeDtypeStruct((R, d), f32),) * 2,
        in_specs=[hbm, hbm, smem, smem],
        out_specs=(vmem, vmem),
        scratch_shapes=[
            pltpu.VMEM((R, d), bf),
            pltpu.VMEM((R, d), bf),
            pltpu.VMEM((8 * R, d), bf),
            pltpu.VMEM((4 * R, d), bf),
            pltpu.VMEM((4 * R, 8 * R), bf),
            pltpu.VMEM((8 * R, 4 * R), bf),
            pltpu.VMEM((4 * R, d), f32),
            pltpu.VMEM((4 * R, d), bf),
            pltpu.VMEM((R + RA, d), bf),
            pltpu.VMEM((R, d), bf),
            pltpu.VMEM((R - RA, d), bf),
            pltpu.VMEM((4 * R, d), f32),
            pltpu.VMEM((4 * R, d), bf),
            pltpu.VMEM((4 * R, d), bf),
            pltpu.VMEM((3 * R, d), bf),
            pltpu.VMEM((R, d), bf),
            pltpu.VMEM((2 * R, d), bf),
            pltpu.SemaphoreType.DMA((2,)),
            pltpu.SemaphoreType.DMA((n_copies,)),
            pltpu.SemaphoreType.DMA((n_copies,)),
        ],
        compiler_params=pltpu.CompilerParams(
            collective_id=0, has_side_effects=True, vmem_limit_bytes=48 * 2**20
        ),
        name="pair_grads",
    )(images, text_embed, log_scale, logit_bias)


def solution(mesh):
    in_specs = (P(("blk", "grp"), None), P(("blk", "grp"), None), P(), P())
    out_specs = (P(("blk", "grp"), None), P(("blk", "grp"), None))
    return jax.shard_map(
        per_device, mesh=mesh, in_specs=in_specs, out_specs=out_specs, check_vma=False
    )
```

time: 519 us -> 64.4 us (0.12)
  waiting for transfers between devices: 468 us -> 0 us
  Pallas kernels: 0 us -> 58.3 us
  matrix products: 24.5 us -> 0 us
  between operations: 15.1 us -> 1.94 us
  other arithmetic: 7.42 us -> 0 us
    reduce_scatter x2 -> x0, waiting for transfers between devices: 277 us -> none  [the longest x1 145 us: per_device(): lax.psum_scatter(own_partial, 'grp', scatter_dimension=0, tiled=True)]
    ppermute x2 -> x0, waiting for transfers between devices: 105 us -> none  [from_behind(): return lax.ppermute(x, axis, [(i, (i + by) % count) for i in range(count)])]
    all_gather x1 -> x0, waiting for transfers between devices: 86.4 us -> none  [per_device(): own_block = lax.all_gather(txt_hat, 'grp', axis=0, tiled=True)]
    pallas_call x0 -> x1, Pallas kernels: none -> 58.3 us  [per_device(): pl.pallas_call(kernel, out_shape=(jax.ShapeDtypeStruct((R, d), f32),) * 2...]
    dot_general x6 -> x0, matrix products: 24.5 us -> none  [the longest x2 7.01 us: pair_weights(): lax.dot_general(rows_here, block, (((1,), (1,)), ((), ())), preferred_ele...]
  transfers between devices with their start and end apart: 5 -> 0, of which waited for: 4 -> 0; matrix products, arithmetic and copies ran while one was open for 4% -> 0% of each run, Pallas kernels for 0% -> 0%
where the time goes in v1:
time: 64.4 us; the launch traced here: 63.8 us
  Pallas kernels  58.3 us (91%)
  local copies, waits for them, and re-layouts  3.55 us (6%)
  between operations  1.94 us (3%)
    pallas_call x1, Pallas kernels, per_device(): pl.pallas_call(kernel, out_shape=(jax.ShapeDtypeStruct((R, d), f32),) * 2...  58.3 us
    unnamed x6, local copies, waits for them, and re-layouts  3.55 us

profile of v1, /device:TPU:1, one launch (start us, length us, event | category | flops | bytes accessed | tf_op | source)
XLA Modules:
  0.0 63.8 jit_solution(17977320193126937616)
XLA Ops:
  1.9 0.0 copy-start
  1.9 1.0 %copy-done = bf16[128,1152]{1,0:T(8,128)(2,1)S(1)} copy-done((bf16[128,1152]{1,0:T(8,128)(2,1)S(1)}, bf16[128,1152]{1,0:T(8,128)(2,1)}, u32[]{:S(2)}) %copy-start) | copy-done | bytes 294936
  2.9 0.0 copy-start.1
  2.9 1.0 %copy-done.1 = bf16[128,1152]{1,0:T(8,128)(2,1)S(1)} copy-done((bf16[128,1152]{1,0:T(8,128)(2,1)S(1)}, bf16[128,1152]{1,0:T(8,128)(2,1)}, u32[]{:S(2)}) %copy-start.1) | copy-done | bytes 294936
  3.8 58.3 %pair_grads.1 = (f32[128,1152]{1,0:T(8,128)S(1)}, f32[128,1152]{1,0:T(8,128)S(1)}) custom-call(bf16[128,1152]{1,0:T(8,128)(2,1)S(1)} %copy-done, bf16[128,1152]{1,0:T(8,128)(2,1)S(1)} %copy-done.1, f32[1]{0:T(128)S(6)} %copy.8.ls_ref, f32[1]{0:T(128)S(6)} %copy.9.lb_ref), custom_call_target="tpu_custom_call" | custom-call | tf_op jit(solution)/shard_map/pair_grads/pallas_call | solution.py:260
  62.2 0.8 %copy.10 = f32[128,1152]{1,0:T(8,128)} copy(f32[128,1152]{1,0:T(8,128)S(1)} %get-tuple-element.4) | data formatting | bytes 1179648
  63.0 0.8 %copy.11 = f32[128,1152]{1,0:T(8,128)} copy(f32[128,1152]{1,0:T(8,128)S(1)} %get-tuple-element.5) | data formatting | bytes 1179648
Async XLA Ops:
  1.9 1.0 %copy-start = (bf16[128,1152]{1,0:T(8,128)(2,1)S(1)}, bf16[128,1152]{1,0:T(8,128)(2,1)}, u32[]{:S(2)}) copy-start(bf16[128,1152]{1,0:T(8,128)(2,1)} %img_hbm.1) | copy-start | bytes 884740
  2.9 1.0 %copy-start.1 = (bf16[128,1152]{1,0:T(8,128)(2,1)S(1)}, bf16[128,1152]{1,0:T(8,128)(2,1)}, u32[]{:S(2)}) copy-start(bf16[128,1152]{1,0:T(8,128)(2,1)} %txt_hbm.1) | copy-start | bytes 884740

commit v2 on v0

v2 whole, which is shorter than its diff:
```python
import jax
import jax.numpy as jnp
from jax import lax
from jax.experimental import pallas as pl
from jax.experimental.pallas import tpu as pltpu
from jax.sharding import PartitionSpec as P

EPS = 1e-06
R = 128
HALF = R // 2
NX, NZ, NBLK = 4, 8, 16

SEGMENTS = (
    ("a", 16, "-", "A"),
    ("b", 32, "-", "A"),
    ("e", 32, "-", "B"),
    ("c", 16, "+", "B"),
    ("d", 32, "+", "B"),
)
BATCHES = (
    (("O", "*"), ("P1", "*")),
    (("P2", "a"), ("P2", "b"), ("P2", "e"), ("Q", "c"), ("Q", "d")),
    (("P2", "c"), ("P2", "d"), ("Q", "a"), ("Q", "b"), ("Q", "e")),
)
PAIRS = {"A": (0, 0), "B": (1, 1), "C": (2, 3), "D": (3, 2)}
ORDER = (
    "f_a", "f_b", "f_e", "n_d", "n_c", "n_e", "r_lo", "l_hi", "r_hi", "l_lo", "t_0", "o_d",
    "o_c", "o_a", "r2", "l2", "n_b", "n_a", "t_3", "t_1", "o_b", "f_d", "t_2", "f_c", "o_e",
    "z1A", "z1D", "z1B", "z1C", "d1", "bof_d", "z0C", "z0D", "bfo_b", "z0B", "bof_c", "bfo_a",
    "z0A", "d0", "z2A", "z2D", "z2C", "z2B", "d2", "bof_e", "j1d", "bn_e", "bf_d", "igD", "igB",
    "c2", "igA", "j1a", "bon_a", "c0", "igC", "c3", "c1", "j1b", "bon_b", "j1c", "bf_c", "bn_c",
    "bn_d", "jx2", "x2l", "x2r", "j1e", "bf_e", "jx3l", "x3l", "jx1h", "x1h", "j2a", "bn_a",
    "jx3h", "x3h", "jx1l", "x1l", "j2b", "bn_b", "finI", "finT",
)


def layout():
    offset, at = {}, 0
    for name, count, _, _ in SEGMENTS:
        offset[name] = (at, count)
        at += count
    place, spans, at = {}, [], 0
    for pieces in BATCHES:
        start = at
        for block, name in pieces:
            if name == "*":
                for other, (low, count) in offset.items():
                    place[block, other] = (at + low, count)
                at += R
            else:
                place[block, name] = (at, offset[name][1])
                at += offset[name][1]
        spans.append((start, at - start))
    return offset, place, spans


def kernel(
    img_hbm, txt_hbm, ls_ref, lb_ref, oimg_ref, otxt_ref,
    raw_img, raw_txt, imgs, txts, w_ref, dt_f, dt_b, join_in, own_in, far_in,
    di_f, di_out, di_in, xs, xh_in, xf_in, in_sem, send_sem, recv_sem,
):
    blk = lax.axis_index("blk")
    grp = lax.axis_index("grp")
    core = lax.rem(grp, 2)
    x = lax.rem(grp // 2, NX)
    z = lax.rem(blk, 4) + 4 * (grp // 8)
    f32, bf = jnp.float32, jnp.bfloat16

    def at(dblk, dz, dx=0, dcore=0):
        new_z = lax.rem(z + dz, NZ)
        new_x = lax.rem(x + dx, NX)
        new_core = lax.rem(core + dcore, 2)
        return (lax.rem(blk + dblk, NBLK), (new_z // 4 * NX + new_x) * 2 + new_core)

    near, near_back = at(1, 1), at(15, 7)
    far, far_back = at(1, 5), at(15, 3)
    right, left, twin = at(0, 0, 1), at(0, 0, 3), at(0, 0, 0, 1)

    loads = [
        pltpu.make_async_copy(src, dst, in_sem.at[i])
        for i, (src, dst) in enumerate(((txt_hbm, raw_txt), (img_hbm, raw_img)))
    ]
    for load in loads:
        load.start()
    barrier = pltpu.get_barrier_semaphore()
    peers = (near, near_back, far, far_back, right, left, twin)
    for peer in peers:
        pl.semaphore_signal(barrier, inc=1, device_id=peer, device_id_type=pl.DeviceIdType.MESH)

    copies, waited = {}, set()

    def send(name, src, dst, to):
        k = len(copies)
        copies[name] = pltpu.make_async_remote_copy(
            src_ref=src, dst_ref=dst, send_sem=send_sem.at[k], recv_sem=recv_sem.at[k],
            device_id=to, device_id_type=pl.DeviceIdType.MESH,
        )
        copies[name].start()

    def arrived(*names):
        for name in names:
            if name not in waited:
                waited.add(name)
                copies[name].wait_recv()

    def rows(ref, span):
        return ref.at[pl.ds(*span)]

    def get(ref, span):
        return ref[span[0] : span[0] + span[1], :]

    def unitize(values):
        values = values.astype(f32)
        inverse = lax.rsqrt(jnp.sum(values * values, axis=-1, keepdims=True) + EPS)
        return values * inverse, inverse

    def project(raw, grad_hat):
        unit, inverse = unitize(raw)
        inner = jnp.sum(grad_hat * unit, axis=-1, keepdims=True)
        return inverse * (grad_hat - inner * unit)

    offset, place, spans = layout()
    steps = {}

    def step(name, needs, run, *args):
        steps[name] = (needs, run, args)

    def step_send(name, needs, *args):
        step(name, needs, send, name, *args)

    for k, _, way, _ in SEGMENTS:
        own, p1, p2, q = (place[block, k] for block in ("O", "P1", "P2", "Q"))
        step_send("n_" + k, (), rows(txts, own), rows(txts, p1), near)
        if way == "+":
            step_send("o_" + k, ("n_" + k,), rows(txts, p1), rows(txts, q), far_back)
            step_send("f_" + k, ("o_" + k,), rows(txts, q), rows(txts, p2), near)
        else:
            step_send("f_" + k, (), rows(txts, own), rows(txts, p2), far)
            step_send("o_" + k, ("f_" + k,), rows(txts, p2), rows(txts, q), near_back)

    def image(dx, part=None, other=0):
        base = next(q for q, d in PAIRS.values() if d == dx) * 2 * R + other * R
        return (base, R) if part is None else (base + part * HALF, HALF)

    def step_image(name, needs, src, dst, to):
        step_send(name, needs, rows(imgs, src), rows(imgs, dst), to)

    step_image("r_lo", (), image(0, 0), image(3, 0), right)
    step_image("l_hi", (), image(0, 1), image(1, 1), left)
    step_image("r_hi", (), image(0, 1), image(3, 1), right)
    step_image("l_lo", (), image(0, 0), image(1, 0), left)
    step_image("r2", ("r_lo",), image(3, 0), image(2, 0), right)
    step_image("l2", ("l_hi",), image(1, 1), image(2, 1), left)
    step_image("t_0", (), image(0), image(0, None, 1), twin)
    step_image("t_3", ("r_lo", "r_hi"), image(3), image(3, None, 1), twin)
    step_image("t_1", ("l_lo", "l_hi"), image(1), image(1, None, 1), twin)
    step_image("t_2", ("r2", "l2"), image(2), image(2, None, 1), twin)
    image_needs = {
        "A": ("t_0",), "B": ("l_lo", "l_hi", "t_1"), "C": ("r_lo", "r_hi", "t_3"), "D": ("r2", "l2", "t_2"),
    }

    def score(start, count, q, labelled):
        logits = lax.dot_general(
            txts[start : start + count, :], imgs[q * 256 : q * 256 + 256, :],
            (((1,), (1,)), ((), ())), preferred_element_type=f32,
        )
        weight = jax.nn.sigmoid(temper * logits + bias)
        if labelled:
            row = lax.broadcasted_iota(jnp.int32, (count, 256), 0)
            col = lax.broadcasted_iota(jnp.int32, (count, 256), 1)
            weight = weight - jnp.logical_and(row == col, row < R).astype(f32)
        w_ref[start : start + count, q * 256 : q * 256 + 256] = (temper * weight).astype(bf)

    def text_grads(start, count):
        grad = jnp.dot(w_ref[start : start + count, :], imgs[...], preferred_element_type=f32)
        dt_f[start : start + count, :] = grad
        dt_b[start : start + count, :] = grad.astype(bf)

    for b, (pieces, (start, count)) in enumerate(zip(BATCHES, spans)):
        needs = ()
        for block, name in pieces:
            if block != "O":
                prefix = {"P1": "n_", "P2": "f_", "Q": "o_"}[block]
                needs += tuple(prefix + k for k in (offset if name == "*" else (name,)))
        for letter, (q, _) in PAIRS.items():
            step("z%d%s" % (b, letter), needs + image_needs[letter], score, start, count, q, (b, q) == (0, 0))
        step("d%d" % b, (), text_grads, start, count)

    def join(span, slot):
        start, count = span
        total = dt_f[start : start + count, :] + get(join_in, slot).astype(f32)
        dt_b[start : start + count, :] = total.astype(bf)

    low = 0
    for k, count, _, way in SEGMENTS:
        own, p1, p2, q = (place[block, k] for block in ("O", "P1", "P2", "Q"))
        slot, slot2 = (low, count), (low + count, count)
        if way == "A":
            low += 2 * count
            step_send("bfo_" + k, (), rows(dt_b, p2), rows(join_in, slot), near_back)
            step("j1" + k, ("bfo_" + k,), join, q, slot)
            step_send("bon_" + k, (), rows(dt_b, q), rows(join_in, slot2), far)
            step("j2" + k, ("bon_" + k,), join, p1, slot2)
        else:
            low += count
            step_send("bof_" + k, (), rows(dt_b, q), rows(join_in, slot), near)
            step("j1" + k, ("bof_" + k,), join, p2, slot)
            step_send("bf_" + k, (), rows(dt_b, p2), rows(far_in, offset[k]), far_back)
        step_send("bn_" + k, (), rows(dt_b, p1), rows(own_in, offset[k]), near_back)

    def final_text():
        for k, _, _, way in SEGMENTS:
            own, here = place["O", k], offset[k]
            total = get(dt_f, own) + get(own_in, here).astype(f32)
            if way == "B":
                total = total + get(far_in, here).astype(f32)
            otxt_ref[here[0] : here[0] + here[1], :] = project(get(raw_txt, here), total)

    step("finT", tuple(("bn_" if way == "A" else "bf_") + k for k, _, _, way in SEGMENTS)
         + tuple("bn_" + k for k, _, _, way in SEGMENTS if way == "B"), final_text)

    def image_grads(q):
        grad = lax.dot_general(
            w_ref[:, q * 256 : q * 256 + 256], txts[...], (((0,), (0,)), ((), ())),
            preferred_element_type=f32,
        )
        di_f[q * R : q * R + R, :] = grad[0:R, :]
        di_out[q * R : q * R + R, :] = grad[R : 2 * R, :].astype(bf)

    block = {dx: q * R for q, dx in PAIRS.values()}

    def both(dx, part=None):
        span = (block[dx], R) if part is None else (block[dx] + part * HALF, HALF)
        return get(di_f, span) + get(di_in, span).astype(f32)

    for letter, (q, dx) in PAIRS.items():
        step("ig" + letter, (), image_grads, q)
        span = (block[dx], R)
        step_send("c%d" % dx, (), rows(di_out, span), rows(di_in, span), twin)

    def stage(dx, part, received=None):
        start = block[dx] + part * HALF
        total = both(dx, part)
        if received is not None:
            total = total + xh_in[received * HALF : received * HALF + HALF, :].astype(f32)
        xs[start : start + HALF, :] = total.astype(bf)

    def stage_two():
        stage(2, 0)
        stage(2, 1)

    def staged(dx, part):
        return rows(xs, (block[dx] + part * HALF, HALF))

    step("jx2", ("c2",), stage_two)
    step_send("x2r", (), staged(2, 0), rows(xh_in, (0, HALF)), right)
    step_send("x2l", (), staged(2, 1), rows(xh_in, (HALF, HALF)), left)
    step("jx1h", ("c1",), stage, 1, 1)
    step_send("x1h", (), staged(1, 1), rows(xf_in, (HALF, HALF)), right)
    step("jx3l", ("c3",), stage, 3, 0)
    step_send("x3l", (), staged(3, 0), rows(xf_in, (R, HALF)), left)
    step("jx1l", ("c1", "x2r"), stage, 1, 0, 0)
    step_send("x1l", (), staged(1, 0), rows(xf_in, (0, HALF)), right)
    step("jx3h", ("c3", "x2l"), stage, 3, 1, 1)
    step_send("x3h", (), staged(3, 1), rows(xf_in, (R + HALF, HALF)), left)

    def final_image():
        total = both(0) + get(xf_in, (0, R)).astype(f32) + get(xf_in, (R, R)).astype(f32)
        oimg_ref[...] = project(raw_img[...], total)

    step("finI", ("c0", "x1h", "x1l", "x3l", "x3h"), final_image)

    loads[0].wait()
    unit, _ = unitize(raw_txt[...])
    txts[0:R, :] = unit.astype(bf)
    loads[1].wait()
    unit, _ = unitize(raw_img[...])
    imgs[0:R, :] = unit.astype(bf)
    temper = jnp.exp(jnp.full((1, 256), ls_ref[0], f32))
    bias = jnp.full((1, 256), lb_ref[0], f32)
    pl.semaphore_wait(barrier, len(peers))

    for name in ORDER:
        needs, run, args = steps[name]
        arrived(*needs)
        run(*args)
    for copy in copies.values():
        copy.wait_send()


def per_device(images, text_embed, log_scale, logit_bias):
    d = images.shape[1]
    bf, f32 = jnp.bfloat16, jnp.float32
    vmem = pl.BlockSpec(memory_space=pltpu.VMEM)
    hbm = pl.BlockSpec(memory_space=pltpu.HBM)
    smem = pl.BlockSpec(memory_space=pltpu.SMEM)
    n_copies = 56
    return pl.pallas_call(
        kernel,
        out_shape=(jax.ShapeDtypeStruct((R, d), f32),) * 2,
        in_specs=[hbm, hbm, smem, smem],
        out_specs=(vmem, vmem),
        scratch_shapes=[
            pltpu.VMEM((R, d), bf),
            pltpu.VMEM((R, d), bf),
            pltpu.VMEM((8 * R, d), bf),
            pltpu.VMEM((4 * R, d), bf),
            pltpu.VMEM((4 * R, 8 * R), bf),
            pltpu.VMEM((4 * R, d), f32),
            pltpu.VMEM((4 * R, d), bf),
            pltpu.VMEM((2 * R, d), bf),
            pltpu.VMEM((R, d), bf),
            pltpu.VMEM((R, d), bf),
            pltpu.VMEM((4 * R, d), f32),
            pltpu.VMEM((4 * R, d), bf),
            pltpu.VMEM((4 * R, d), bf),
            pltpu.VMEM((4 * R, d), bf),
            pltpu.VMEM((R, d), bf),
            pltpu.VMEM((2 * R, d), bf),
            pltpu.SemaphoreType.DMA((2,)),
            pltpu.SemaphoreType.DMA((n_copies,)),
            pltpu.SemaphoreType.DMA((n_copies,)),
        ],
        compiler_params=pltpu.CompilerParams(
            collective_id=0, has_side_effects=True, vmem_limit_bytes=48 * 2**20
        ),
        name="pair_grads",
    )(images, text_embed, log_scale, logit_bias)


def solution(mesh):
    in_specs = (P(("blk", "grp"), None), P(("blk", "grp"), None), P(), P())
    out_specs = (P(("blk", "grp"), None), P(("blk", "grp"), None))
    return jax.shard_map(
        per_device, mesh=mesh, in_specs=in_specs, out_specs=out_specs, check_vma=False
    )
```

time: 519 us -> 55.7 us (0.11)
  waiting for transfers between devices: 468 us -> 0 us
  Pallas kernels: 0 us -> 50.1 us
  matrix products: 24.5 us -> 0 us
  between operations: 15.1 us -> 1.94 us
  other arithmetic: 7.42 us -> 0 us
    reduce_scatter x2 -> x0, waiting for transfers between devices: 277 us -> none  [the longest x1 145 us: per_device(): lax.psum_scatter(own_partial, 'grp', scatter_dimension=0, tiled=True)]
    ppermute x2 -> x0, waiting for transfers between devices: 105 us -> none  [from_behind(): return lax.ppermute(x, axis, [(i, (i + by) % count) for i in range(count)])]
    all_gather x1 -> x0, waiting for transfers between devices: 86.4 us -> none  [per_device(): own_block = lax.all_gather(txt_hat, 'grp', axis=0, tiled=True)]
    pallas_call x0 -> x1, Pallas kernels: none -> 50.1 us  [per_device(): pl.pallas_call(kernel, out_shape=(jax.ShapeDtypeStruct((R, d), f32),) * 2...]
    dot_general x6 -> x0, matrix products: 24.5 us -> none  [the longest x2 7.01 us: pair_weights(): lax.dot_general(rows_here, block, (((1,), (1,)), ((), ())), preferred_ele...]
  transfers between devices with their start and end apart: 5 -> 0, of which waited for: 4 -> 0; matrix products, arithmetic and copies ran while one was open for 4% -> 0% of each run, Pallas kernels for 0% -> 0%
where the time goes in v2:
time: 55.7 us; the launch traced here: 55.6 us
  Pallas kernels  50.1 us (90%)
  local copies, waits for them, and re-layouts  3.55 us (6%)
  between operations  1.94 us (3%)
    pallas_call x1, Pallas kernels, per_device(): pl.pallas_call(kernel, out_shape=(jax.ShapeDtypeStruct((R, d), f32),) * 2...  50.1 us
    unnamed x6, local copies, waits for them, and re-layouts  3.55 us

profile of v2, /device:TPU:1, one launch (start us, length us, event | category | flops | bytes accessed | tf_op | source)
XLA Modules:
  0.0 55.6 jit_solution(7457822899154479901)
XLA Ops:
  1.9 0.0 copy-start
  1.9 1.0 %copy-done = bf16[128,1152]{1,0:T(8,128)(2,1)S(1)} copy-done((bf16[128,1152]{1,0:T(8,128)(2,1)S(1)}, bf16[128,1152]{1,0:T(8,128)(2,1)}, u32[]{:S(2)}) %copy-start) | copy-done | bytes 294936
  2.9 0.0 copy-start.1
  2.9 1.0 %copy-done.1 = bf16[128,1152]{1,0:T(8,128)(2,1)S(1)} copy-done((bf16[128,1152]{1,0:T(8,128)(2,1)S(1)}, bf16[128,1152]{1,0:T(8,128)(2,1)}, u32[]{:S(2)}) %copy-start.1) | copy-done | bytes 294936
  3.8 50.1 %pair_grads.1 = (f32[128,1152]{1,0:T(8,128)S(1)}, f32[128,1152]{1,0:T(8,128)S(1)}) custom-call(bf16[128,1152]{1,0:T(8,128)(2,1)S(1)} %copy-done, bf16[128,1152]{1,0:T(8,128)(2,1)S(1)} %copy-done.1, f32[1]{0:T(128)S(6)} %copy.8.ls_ref, f32[1]{0:T(128)S(6)} %copy.9.lb_ref), custom_call_target="tpu_custom_call" | custom-call | tf_op jit(solution)/shard_map/pair_grads/pallas_call | solution.py:298
  53.9 0.8 %copy.10 = f32[128,1152]{1,0:T(8,128)} copy(f32[128,1152]{1,0:T(8,128)S(1)} %get-tuple-element.4) | data formatting | bytes 1179648
  54.8 0.8 %copy.11 = f32[128,1152]{1,0:T(8,128)} copy(f32[128,1152]{1,0:T(8,128)S(1)} %get-tuple-element.5) | data formatting | bytes 1179648
Async XLA Ops:
  1.9 1.0 %copy-start = (bf16[128,1152]{1,0:T(8,128)(2,1)S(1)}, bf16[128,1152]{1,0:T(8,128)(2,1)}, u32[]{:S(2)}) copy-start(bf16[128,1152]{1,0:T(8,128)(2,1)} %img_hbm.1) | copy-start | bytes 884740
  2.9 1.0 %copy-start.1 = (bf16[128,1152]{1,0:T(8,128)(2,1)S(1)}, bf16[128,1152]{1,0:T(8,128)(2,1)}, u32[]{:S(2)}) copy-start(bf16[128,1152]{1,0:T(8,128)(2,1)} %txt_hbm.1) | copy-start | bytes 884740

commit v3 on v2

--- a/solution.py
+++ b/solution.py
@@ -13,24 +13,27 @@
 SEGMENTS = (
     ("a", 16, "-", "A"),
     ("b", 32, "-", "A"),
-    ("e", 32, "-", "B"),
+    ("e", 16, "-", "B"),
+    ("h", 16, "-", "B"),
     ("c", 16, "+", "B"),
     ("d", 32, "+", "B"),
 )
 BATCHES = (
     (("O", "*"), ("P1", "*")),
-    (("P2", "a"), ("P2", "b"), ("P2", "e"), ("Q", "c"), ("Q", "d")),
-    (("P2", "c"), ("P2", "d"), ("Q", "a"), ("Q", "b"), ("Q", "e")),
+    (("P2", "a"), ("P2", "b"), ("P2", "e"), ("P2", "h"), ("Q", "c"), ("Q", "d")),
+    (("P2", "c"), ("Q", "a"), ("Q", "b")),
+    (("P2", "d"), ("Q", "e"), ("Q", "h")),
 )
 PAIRS = {"A": (0, 0), "B": (1, 1), "C": (2, 3), "D": (3, 2)}
 ORDER = (
-    "f_a", "f_b", "f_e", "n_d", "n_c", "n_e", "r_lo", "l_hi", "r_hi", "l_lo", "t_0", "o_d",
-    "o_c", "o_a", "r2", "l2", "n_b", "n_a", "t_3", "t_1", "o_b", "f_d", "t_2", "f_c", "o_e",
-    "z1A", "z1D", "z1B", "z1C", "d1", "bof_d", "z0C", "z0D", "bfo_b", "z0B", "bof_c", "bfo_a",
-    "z0A", "d0", "z2A", "z2D", "z2C", "z2B", "d2", "bof_e", "j1d", "bn_e", "bf_d", "igD", "igB",
-    "c2", "igA", "j1a", "bon_a", "c0", "igC", "c3", "c1", "j1b", "bon_b", "j1c", "bf_c", "bn_c",
-    "bn_d", "jx2", "x2l", "x2r", "j1e", "bf_e", "jx3l", "x3l", "jx1h", "x1h", "j2a", "bn_a",
-    "jx3h", "x3h", "jx1l", "x1l", "j2b", "bn_b", "finI", "finT",
+    "f_h", "n_d", "n_c", "n_h", "f_e", "n_b", "f_b", "r_lo", "l_hi", "t_0", "f_a", "r_hi",
+    "l_lo", "o_d", "o_c", "o_h", "l2", "r2", "o_e", "t_3", "t_1", "n_a", "o_b", "t_2", "f_d",
+    "o_a", "f_c", "z1B", "n_e", "z1A", "z1D", "z1C", "d1", "bof_c", "bof_d", "bfo_a", "z3C",
+    "z3A", "z3B", "z3D", "bfo_b", "d3", "bof_h", "z2B", "z2D", "z2A", "z2C", "d2", "j1a",
+    "bon_a", "j1c", "bf_c", "z0D", "igD", "c2", "z0C", "igC", "j1d", "bof_e", "c3", "bf_d",
+    "j1b", "bon_b", "j1h", "z0B", "igB", "c1", "jx2", "x2l", "x2r", "z0A", "d0", "bn_h", "igA",
+    "bn_e", "j2a", "c0", "jx3l", "j1e", "bf_e", "x3l", "bn_c", "bf_h", "jx1h", "x1h", "bn_d",
+    "jx3h", "jx1l", "x1l", "x3h", "j2b", "bn_b", "bn_a", "finI", "finT",
 )
 
 
@@ -55,9 +58,9 @@
 
 
 def kernel(
-    img_hbm, txt_hbm, ls_ref, lb_ref, oimg_ref, otxt_ref,
-    raw_img, raw_txt, imgs, txts, w_ref, dt_f, dt_b, join_in, own_in, far_in,
-    di_f, di_out, di_in, xs, xh_in, xf_in, in_sem, send_sem, recv_sem,
+    raw, ls_ref, lb_ref, oimg_ref, otxt_ref,
+    imgs, txts, w_ref, dt_f, dt_b, join_in, own_in, far_in,
+    di_f, di_out, di_in, xs, xh_in, xf_in, send_sem, recv_sem,
 ):
     blk = lax.axis_index("blk")
     grp = lax.axis_index("grp")
@@ -76,12 +79,6 @@
     far, far_back = at(1, 5), at(15, 3)
     right, left, twin = at(0, 0, 1), at(0, 0, 3), at(0, 0, 0, 1)
 
-    loads = [
-        pltpu.make_async_copy(src, dst, in_sem.at[i])
-        for i, (src, dst) in enumerate(((txt_hbm, raw_txt), (img_hbm, raw_img)))
-    ]
-    for load in loads:
-        load.start()
     barrier = pltpu.get_barrier_semaphore()
     peers = (near, near_back, far, far_back, right, left, twin)
     for peer in peers:
@@ -214,7 +211,7 @@
             total = get(dt_f, own) + get(own_in, here).astype(f32)
             if way == "B":
                 total = total + get(far_in, here).astype(f32)
-            otxt_ref[here[0] : here[0] + here[1], :] = project(get(raw_txt, here), total)
+            otxt_ref[here[0] : here[0] + here[1], :] = project(get(raw, here), total)
 
     step("finT", tuple(("bn_" if way == "A" else "bf_") + k for k, _, _, way in SEGMENTS)
          + tuple("bn_" + k for k, _, _, way in SEGMENTS if way == "B"), final_text)
@@ -266,18 +263,16 @@
 
     def final_image():
         total = both(0) + get(xf_in, (0, R)).astype(f32) + get(xf_in, (R, R)).astype(f32)
-        oimg_ref[...] = project(raw_img[...], total)
+        oimg_ref[...] = project(get(raw, (R, R)), total)
 
     step("finI", ("c0", "x1h", "x1l", "x3l", "x3h"), final_image)
 
-    loads[0].wait()
-    unit, _ = unitize(raw_txt[...])
+    unit, _ = unitize(raw[0:R, :])
     txts[0:R, :] = unit.astype(bf)
-    loads[1].wait()
-    unit, _ = unitize(raw_img[...])
+    unit, _ = unitize(raw[R : 2 * R, :])
     imgs[0:R, :] = unit.astype(bf)
-    temper = jnp.exp(jnp.full((1, 256), ls_ref[0], f32))
-    bias = jnp.full((1, 256), lb_ref[0], f32)
+    temper = jnp.exp(jnp.broadcast_to(ls_ref[...], (1, 256)))
+    bias = jnp.broadcast_to(lb_ref[...], (1, 256))
     pl.semaphore_wait(barrier, len(peers))
 
     for name in ORDER:
@@ -292,17 +287,14 @@
     d = images.shape[1]
     bf, f32 = jnp.bfloat16, jnp.float32
     vmem = pl.BlockSpec(memory_space=pltpu.VMEM)
-    hbm = pl.BlockSpec(memory_space=pltpu.HBM)
-    smem = pl.BlockSpec(memory_space=pltpu.SMEM)
-    n_copies = 56
+    raw = jnp.concatenate([text_embed, images], axis=0)
+    n_copies = 64
     return pl.pallas_call(
         kernel,
         out_shape=(jax.ShapeDtypeStruct((R, d), f32),) * 2,
-        in_specs=[hbm, hbm, smem, smem],
+        in_specs=[vmem, vmem, vmem],
         out_specs=(vmem, vmem),
         scratch_shapes=[
-            pltpu.VMEM((R, d), bf),
-            pltpu.VMEM((R, d), bf),
             pltpu.VMEM((8 * R, d), bf),
             pltpu.VMEM((4 * R, d), bf),
             pltpu.VMEM((4 * R, 8 * R), bf),
@@ -317,7 +309,6 @@
             pltpu.VMEM((4 * R, d), bf),
             pltpu.VMEM((R, d), bf),
             pltpu.VMEM((2 * R, d), bf),
-            pltpu.SemaphoreType.DMA((2,)),
             pltpu.SemaphoreType.DMA((n_copies,)),
             pltpu.SemaphoreType.DMA((n_copies,)),
         ],
@@ -325,7 +316,7 @@
             collective_id=0, has_side_effects=True, vmem_limit_bytes=48 * 2**20
         ),
         name="pair_grads",
-    )(images, text_embed, log_scale, logit_bias)
+    )(raw, log_scale.reshape(1, 1), logit_bias.reshape(1, 1))
 
 
 def solution(mesh):

time: 55.7 us -> 54.7 us (0.982)
  local copies, waits for them, and re-layouts: 3.55 us -> 1.63 us
  other arithmetic: 0 us -> 1.1 us
    unnamed x6 -> x2, local copies, waits for them, and re-layouts: 3.55 us -> 1.63 us
    concatenate x0 -> x1, other arithmetic: none -> 1.1 us  [per_device(): raw = jnp.concatenate([text_embed, images], axis=0)]
where the time goes in v3:
time: 54.7 us; the launch traced here: 54.6 us
  Pallas kernels  50 us (91%)
  between operations  1.93 us (4%)
  local copies, waits for them, and re-layouts  1.63 us (3%)
  other arithmetic  1.1 us (2%)
    pallas_call x1, Pallas kernels, per_device(): pl.pallas_call(kernel, out_shape=(jax.ShapeDtypeStruct((R, d), f32),) * 2...  50 us
    unnamed x2, local copies, waits for them, and re-layouts  1.63 us
    concatenate x1, other arithmetic, per_device(): raw = jnp.concatenate([text_embed, images], axis=0)  1.1 us

profile of v3, /device:TPU:1, one launch (start us, length us, event | category | flops | bytes accessed | tf_op | source)
XLA Modules:
  0.0 54.6 jit_solution(11601395441103709666)
XLA Ops:
  1.9 1.1 %pad_maximum_fusion.raw = bf16[256,1152]{1,0:T(8,128)(2,1)S(1)} fusion(bf16[128,1152]{1,0:T(8,128)(2,1)} %param.4, bf16[128,1152]{1,0:T(8,128)(2,1)} %param.5), kind=kLoop, calls=%fused_computation | loop fusion | flops 1179648 | bytes 1179648 | tf_op jit(solution)/shard_map/concatenate | solution.py:290
  3.0 50.0 %pair_grads.1 = (f32[128,1152]{1,0:T(8,128)S(1)}, f32[128,1152]{1,0:T(8,128)S(1)}) custom-call(bf16[256,1152]{1,0:T(8,128)(2,1)S(1)} %pad_maximum_fusion.raw, f32[1,1]{1,0:T(1,128)} %bitcast.2.ls_ref, f32[1,1]{1,0:T(1,128)} %bitcast.3.lb_ref), custom_call_target="tpu_custom_call" | custom-call | tf_op jit(solution)/shard_map/pair_grads/pallas_call | solution.py:292
  53.0 0.8 %copy.10 = f32[128,1152]{1,0:T(8,128)} copy(f32[128,1152]{1,0:T(8,128)S(1)} %get-tuple-element.4) | data formatting | bytes 1179648
  53.8 0.8 %copy.11 = f32[128,1152]{1,0:T(8,128)} copy(f32[128,1152]{1,0:T(8,128)S(1)} %get-tuple-element.5) | data formatting | bytes 1179648

commit v4 on v3

--- a/solution.py
+++ b/solution.py
@@ -21,19 +21,18 @@
 BATCHES = (
     (("O", "*"), ("P1", "*")),
     (("P2", "a"), ("P2", "b"), ("P2", "e"), ("P2", "h"), ("Q", "c"), ("Q", "d")),
-    (("P2", "c"), ("Q", "a"), ("Q", "b")),
-    (("P2", "d"), ("Q", "e"), ("Q", "h")),
+    (("P2", "c"), ("P2", "d"), ("Q", "a"), ("Q", "b"), ("Q", "e"), ("Q", "h")),
 )
 PAIRS = {"A": (0, 0), "B": (1, 1), "C": (2, 3), "D": (3, 2)}
 ORDER = (
-    "f_h", "n_d", "n_c", "n_h", "f_e", "n_b", "f_b", "r_lo", "l_hi", "t_0", "f_a", "r_hi",
-    "l_lo", "o_d", "o_c", "o_h", "l2", "r2", "o_e", "t_3", "t_1", "n_a", "o_b", "t_2", "f_d",
-    "o_a", "f_c", "z1B", "n_e", "z1A", "z1D", "z1C", "d1", "bof_c", "bof_d", "bfo_a", "z3C",
-    "z3A", "z3B", "z3D", "bfo_b", "d3", "bof_h", "z2B", "z2D", "z2A", "z2C", "d2", "j1a",
-    "bon_a", "j1c", "bf_c", "z0D", "igD", "c2", "z0C", "igC", "j1d", "bof_e", "c3", "bf_d",
-    "j1b", "bon_b", "j1h", "z0B", "igB", "c1", "jx2", "x2l", "x2r", "z0A", "d0", "bn_h", "igA",
-    "bn_e", "j2a", "c0", "jx3l", "j1e", "bf_e", "x3l", "bn_c", "bf_h", "jx1h", "x1h", "bn_d",
-    "jx3h", "jx1l", "x1l", "x3h", "j2b", "bn_b", "bn_a", "finI", "finT",
+    "n_c", "n_d", "f_e", "l_hi", "r_lo", "n_a", "f_a", "f_h", "l_lo", "t_0", "r_hi", "o_c",
+    "o_d", "f_b", "l2", "r2", "n_h", "t_1", "n_e", "t_2", "n_b", "o_a", "o_e", "o_h", "t_3",
+    "f_c", "f_d", "o_b", "z1D", "z1A", "z1B", "z1C", "d1", "bof_d", "bfo_b", "bof_c", "z0B",
+    "z0C", "bfo_a", "z0D", "z2A", "z2D", "z2B", "z2C", "d2", "bof_e", "j1b", "bon_b", "j1d",
+    "bf_d", "igD", "c2", "igB", "c1", "bof_h", "j1a", "igC", "z0A", "igA", "jx2", "x2r", "x2l",
+    "bon_a", "c3", "j1e", "jx3l", "jx1h", "x1h", "x3l", "bf_e", "d0", "bn_h", "bn_c", "bn_e",
+    "j1h", "j1c", "jx3h", "bf_h", "bn_d", "jx1l", "x1l", "j2a", "bf_c", "x3h", "bn_a", "j2b",
+    "c0", "bn_b", "finI", "finT",
 )
 
 

time: 54.7 us -> 52.8 us (0.965)
  Pallas kernels: 50 us -> 48 us
    pallas_call x1, Pallas kernels: 50 us -> 48 us  [per_device(): pl.pallas_call(kernel, out_shape=(jax.ShapeDtypeStruct((R, d), f32),) * 2...]
where the time goes in v4:
time: 52.8 us; the launch traced here: 52.7 us
  Pallas kernels  48 us (91%)
  between operations  1.93 us (4%)
  local copies, waits for them, and re-layouts  1.63 us (3%)
  other arithmetic  1.1 us (2%)
    pallas_call x1, Pallas kernels, per_device(): pl.pallas_call(kernel, out_shape=(jax.ShapeDtypeStruct((R, d), f32),) * 2...  48 us
    unnamed x2, local copies, waits for them, and re-layouts  1.63 us
    concatenate x1, other arithmetic, per_device(): raw = jnp.concatenate([text_embed, images], axis=0)  1.1 us

profile of v4, /device:TPU:1, one launch (start us, length us, event | category | flops | bytes accessed | tf_op | source)
XLA Modules:
  0.0 52.7 jit_solution(3830975306558496974)
XLA Ops:
  1.9 1.1 %pad_maximum_fusion.raw = bf16[256,1152]{1,0:T(8,128)(2,1)S(1)} fusion(bf16[128,1152]{1,0:T(8,128)(2,1)} %param.4, bf16[128,1152]{1,0:T(8,128)(2,1)} %param.5), kind=kLoop, calls=%fused_computation | loop fusion | flops 1179648 | bytes 1179648 | tf_op jit(solution)/shard_map/concatenate | solution.py:289
  3.0 48.0 %pair_grads.1 = (f32[128,1152]{1,0:T(8,128)S(1)}, f32[128,1152]{1,0:T(8,128)S(1)}) custom-call(bf16[256,1152]{1,0:T(8,128)(2,1)S(1)} %pad_maximum_fusion.raw, f32[1,1]{1,0:T(1,128)} %bitcast.2.ls_ref, f32[1,1]{1,0:T(1,128)} %bitcast.3.lb_ref), custom_call_target="tpu_custom_call" | custom-call | tf_op jit(solution)/shard_map/pair_grads/pallas_call | solution.py:291
  51.0 0.8 %copy.10 = f32[128,1152]{1,0:T(8,128)} copy(f32[128,1152]{1,0:T(8,128)S(1)} %get-tuple-element.4) | data formatting | bytes 1179648
  51.9 0.8 %copy.11 = f32[128,1152]{1,0:T(8,128)} copy(f32[128,1152]{1,0:T(8,128)S(1)} %get-tuple-element.5) | data formatting | bytes 1179648

commit v5 on v3

--- a/solution.py
+++ b/solution.py
@@ -26,14 +26,14 @@
 )
 PAIRS = {"A": (0, 0), "B": (1, 1), "C": (2, 3), "D": (3, 2)}
 ORDER = (
-    "f_h", "n_d", "n_c", "n_h", "f_e", "n_b", "f_b", "r_lo", "l_hi", "t_0", "f_a", "r_hi",
-    "l_lo", "o_d", "o_c", "o_h", "l2", "r2", "o_e", "t_3", "t_1", "n_a", "o_b", "t_2", "f_d",
-    "o_a", "f_c", "z1B", "n_e", "z1A", "z1D", "z1C", "d1", "bof_c", "bof_d", "bfo_a", "z3C",
-    "z3A", "z3B", "z3D", "bfo_b", "d3", "bof_h", "z2B", "z2D", "z2A", "z2C", "d2", "j1a",
-    "bon_a", "j1c", "bf_c", "z0D", "igD", "c2", "z0C", "igC", "j1d", "bof_e", "c3", "bf_d",
-    "j1b", "bon_b", "j1h", "z0B", "igB", "c1", "jx2", "x2l", "x2r", "z0A", "d0", "bn_h", "igA",
-    "bn_e", "j2a", "c0", "jx3l", "j1e", "bf_e", "x3l", "bn_c", "bf_h", "jx1h", "x1h", "bn_d",
-    "jx3h", "jx1l", "x1l", "x3h", "j2b", "bn_b", "bn_a", "finI", "finT",
+    "n_c", "f_a", "r_lo", "n_d", "f_h", "l_hi", "n_e", "r_hi", "t_0", "l_lo", "o_c", "f_b",
+    "n_a", "o_d", "r2", "l2", "t_3", "n_h", "t_1", "f_e", "o_b", "n_b", "t_2", "o_a", "f_c",
+    "o_h", "f_d", "z1B", "o_e", "z1D", "z1C", "z1A", "d1", "bfo_b", "bof_c", "z0D", "bof_d",
+    "z2A", "z2C", "z0B", "bfo_a", "z2D", "z2B", "d2", "z3D", "igD", "c2", "z3B", "j1c", "bf_c",
+    "z3C", "j1b", "bon_b", "z3A", "z0C", "d3", "bof_h", "igC", "j1a", "c3", "bon_a", "igB",
+    "jx2", "x2r", "bof_e", "x2l", "c1", "j1d", "bf_d", "z0A", "igA", "jx3l", "x3l", "jx1h",
+    "x1h", "d0", "bn_c", "bn_d", "c0", "j1e", "bf_e", "jx1l", "x1l", "bn_h", "jx3h", "x3h",
+    "j2a", "bn_e", "j2b", "j1h", "bn_a", "bf_h", "bn_b", "finI", "finT",
 )
 
 

time: 54.7 us -> 52.8 us (0.965)
  Pallas kernels: 50 us -> 48 us
    pallas_call x1, Pallas kernels: 50 us -> 48 us  [per_device(): pl.pallas_call(kernel, out_shape=(jax.ShapeDtypeStruct((R, d), f32),) * 2...]
where the time goes in v5:
time: 52.8 us; the launch traced here: 52.7 us
  Pallas kernels  48 us (91%)
  between operations  1.93 us (4%)
  local copies, waits for them, and re-layouts  1.63 us (3%)
  other arithmetic  1.1 us (2%)
    pallas_call x1, Pallas kernels, per_device(): pl.pallas_call(kernel, out_shape=(jax.ShapeDtypeStruct((R, d), f32),) * 2...  48 us
    unnamed x2, local copies, waits for them, and re-layouts  1.63 us
    concatenate x1, other arithmetic, per_device(): raw = jnp.concatenate([text_embed, images], axis=0)  1.1 us

profile of v5, /device:TPU:1, one launch (start us, length us, event | category | flops | bytes accessed | tf_op | source)
XLA Modules:
  0.0 52.7 jit_solution(6306977640917391840)
XLA Ops:
  1.9 1.1 %pad_maximum_fusion.raw = bf16[256,1152]{1,0:T(8,128)(2,1)S(1)} fusion(bf16[128,1152]{1,0:T(8,128)(2,1)} %param.4, bf16[128,1152]{1,0:T(8,128)(2,1)} %param.5), kind=kLoop, calls=%fused_computation | loop fusion | flops 1179648 | bytes 1179648 | tf_op jit(solution)/shard_map/concatenate | solution.py:290
  3.0 48.0 %pair_grads.1 = (f32[128,1152]{1,0:T(8,128)S(1)}, f32[128,1152]{1,0:T(8,128)S(1)}) custom-call(bf16[256,1152]{1,0:T(8,128)(2,1)S(1)} %pad_maximum_fusion.raw, f32[1,1]{1,0:T(1,128)} %bitcast.2.ls_ref, f32[1,1]{1,0:T(1,128)} %bitcast.3.lb_ref), custom_call_target="tpu_custom_call" | custom-call | tf_op jit(solution)/shard_map/pair_grads/pallas_call | solution.py:292
  51.1 0.8 %copy.10 = f32[128,1152]{1,0:T(8,128)} copy(f32[128,1152]{1,0:T(8,128)S(1)} %get-tuple-element.4) | data formatting | bytes 1179648
  51.9 0.8 %copy.11 = f32[128,1152]{1,0:T(8,128)} copy(f32[128,1152]{1,0:T(8,128)S(1)} %get-tuple-element.5) | data formatting | bytes 1179648
